TPU v7x, 256 devices: a whole 4x4x8 slice. The times are simulated.
256 devices in a mesh: tm: 4 (over y), seq: 64 (over x, z, core).
Axes of the slice: x: 4, y: 4, z: 8, core: 2. Of those that a mesh axis runs over, the one named last changes fastest.
Arguments:
- queries: bfloat16 [12288, 4096], P(('tm', 'seq'))
- keys: bfloat16 [12288, 4096], P(('tm', 'seq'))
- values: bfloat16 [12288, 4096], P(('tm', 'seq')), may hold values from -6 to 6
- span_rank: int32 [4], replicated, may hold values from 0 to 3, each once
- token_counts: int32 [4], replicated, may hold values from 1536 to 3072, as said below
Outputs:
- attended: bfloat16 [12288, 4096], P(('tm', 'seq'))
Inputs may be any that keep to these rules, and one draw needn't show every extreme that they name: Each span's valid tokens are its first token_counts slots; at least one span is full.
All inputs are finite; a program needn't handle non-finite values.
Results may differ from a plain program's by a relative error of at most 0.009.
Values may be sent and summed in bfloat16 or wider, within the bound.
A program may use at most 64 MiB of HBM per device.

v0:
```python
import jax
import jax.numpy as jnp
from jax import lax
from jax.sharding import PartitionSpec as P

HS = 128


def local(queries, keys, values, span_rank, token_counts):
    seq_count = lax.axis_size("seq")
    tok_rows = queries.shape[0]
    width = queries.shape[1]
    head_total = width // HS
    query_parts = max(1, seq_count // head_total)
    head_dev = max(1, head_total // seq_count)
    head_groups = head_total // head_dev
    part_rows = tok_rows // query_parts
    score_scale = HS ** (-0.5)
    my_group = lax.axis_index("tm")
    query_split = queries.reshape(query_parts, part_rows, head_groups, head_dev, HS)
    query_split = query_split.transpose(1, 2, 0, 3, 4).reshape(part_rows, seq_count, head_dev, HS)
    query_heads = lax.all_to_all(query_split, "seq", split_axis=1, concat_axis=0, tiled=True)
    query_count = seq_count * part_rows
    query_heads = query_heads.reshape(query_count, head_dev, HS)
    key_rows = seq_count * tok_rows
    block_rows = 512
    block_count = key_rows // block_rows
    positions = jnp.arange(key_rows, dtype=jnp.int32)
    initial = (
        jnp.full((query_count, head_dev), -1e30, jnp.float32),
        jnp.zeros((query_count, head_dev), jnp.float32),
        jnp.zeros((query_count, head_dev, HS), jnp.float32),
    )
    key_all, value_all = (
        lax.all_gather(keys[None], "tm", axis=0, tiled=True),
        lax.all_gather(values[None], "tm", axis=0, tiled=True),
    )
    span_total = key_all.shape[0]

    def spread_all(source):
        wide = jnp.broadcast_to(
            source.reshape(span_total, tok_rows, head_groups, 1, head_dev, HS),
            (span_total, tok_rows, head_groups, query_parts, head_dev, HS),
        )
        return wide.reshape(span_total, tok_rows, seq_count, head_dev, HS)

    key_heads, value_heads = (
        lax.all_to_all(spread_all(key_all), "seq", split_axis=2, concat_axis=1, tiled=True),
        lax.all_to_all(spread_all(value_all), "seq", split_axis=2, concat_axis=1, tiled=True),
    )
    key_heads = key_heads.reshape(span_total, key_rows, head_dev, HS)
    value_heads = value_heads.reshape(span_total, key_rows, head_dev, HS)
    state = initial
    for span_id in range(span_total):
        carried = state
        attend_key_heads = key_heads[span_id]
        attend_value_heads = value_heads[span_id]
        allowed = span_rank[span_id] <= span_rank[my_group]
        valid_count = token_counts[span_id]

        def attend_all(state):

            def advance(index, inner):
                running, total, accum = inner
                key_block = lax.dynamic_slice_in_dim(
                    attend_key_heads, index * block_rows, block_rows, 0
                )
                value_block = lax.dynamic_slice_in_dim(
                    attend_value_heads, index * block_rows, block_rows, 0
                )
                live = (
                    lax.dynamic_slice_in_dim(positions, index * block_rows, block_rows, 0)
                    < valid_count
                )
                scores = (
                    jnp.einsum(
                        "qhd,khd->qhk", query_heads, key_block, preferred_element_type=jnp.float32
                    )
                    * score_scale
                )
                scores = jnp.where(live, scores, -1e30)
                upper = jnp.maximum(running, jnp.max(scores, axis=2))
                weights = jnp.where(live, jnp.exp(scores - upper[..., None]), 0.0)
                rescale = jnp.exp(running - upper)
                total = total * rescale + jnp.sum(weights, axis=2)
                accum = accum * rescale[..., None] + jnp.einsum(
                    "qhk,khd->qhd",
                    weights.astype(jnp.bfloat16),
                    value_block,
                    preferred_element_type=jnp.float32,
                )
                return (upper, total, accum)

            return lax.fori_loop(0, block_count, advance, state)

        def unchanged(state):
            return state

        state = lax.cond(allowed, attend_all, unchanged, carried)
    running, total, accum = state
    result = (accum / total[..., None]).astype(jnp.bfloat16)
    result = result.reshape(query_count, 1, head_dev, HS)
    returned = lax.all_to_all(result, "seq", split_axis=0, concat_axis=1, tiled=True)
    returned = returned.reshape(part_rows, head_groups, query_parts, head_dev, HS)
    return returned.transpose(2, 0, 1, 3, 4).reshape(tok_rows, width)


def solution(mesh):
    return jax.shard_map(
        local,
        mesh=mesh,
        in_specs=(P(("tm", "seq"), None), P(("tm", "seq"), None), P(("tm", "seq"), None), P(), P()),
        out_specs=P(("tm", "seq"), None),
        check_vma=False,
    )
```

profile of v0, /device:TPU:23, one launch (start us, length us, event | category | flops | bytes accessed | tf_op | source)
XLA Modules:
  0.0 472.3 jit_solution(8013672560090010624)
XLA Ops:
  7.3 32.0 %all-gather.5.cloned.1.call-done = bf16[192,4096]{1,0:T(8,128)(2,1)} async-done(((bf16[48,4096]{1,0:T(8,128)(2,1)}), bf16[192,4096]{1,0:T(8,128)(2,1)}) %all-gather.5.cloned.1.call-update) | async-done | bytes 1572880 | tf_op jit(solution)/shard_map/all_gather | solution.py:35
  44.2 11.6 %all-to-all-start = ((bf16[4,48,64,1,128]{4,1,0,3,2:T(8,128)(2,1)}), bf16[4,48,64,1,128]{4,1,0,3,2:T(8,128)(2,1)S(1)}, u32[]{:S(2)}, u32[]{:S(2)}) async-start(bf16[4,48,64,1,128]{4,1,0,3,2:T(8,128)(2,1)} %bitcast.217), calls=%async_computation | async-start | bytes 6291456 | tf_op jit(solution)/shard_map/all_to_all | solution.py:48
  56.6 29.8 %all-gather.7.cloned.1.call-done = bf16[192,4096]{1,0:T(8,128)(2,1)} async-done(((bf16[48,4096]{1,0:T(8,128)(2,1)}), bf16[192,4096]{1,0:T(8,128)(2,1)}) %all-gather.7.cloned.1.call-update) | async-done | bytes 1572880 | tf_op jit(solution)/shard_map/all_gather | solution.py:36
  89.9 39.3 %all-to-all-done = bf16[4,48,64,1,128]{4,1,0,3,2:T(8,128)(2,1)S(1)} async-done(((bf16[4,48,64,1,128]{4,1,0,3,2:T(8,128)(2,1)}), bf16[4,48,64,1,128]{4,1,0,3,2:T(8,128)(2,1)S(1)}, u32[]{:S(2)}, u32[]{:S(2)}) %all-to-all-start) | async-done | bytes 3145760 | tf_op jit(solution)/shard_map/all_to_all | solution.py:48
  129.2 4.0 broadcast_in_dim.171
  133.2 6.5 %all-to-all-start.2 = ((bf16[4,48,64,1,128]{4,1,0,3,2:T(8,128)(2,1)}), bf16[4,48,64,1,128]{4,1,0,3,2:T(8,128)(2,1)}, u32[]{:S(2)}, u32[]{:S(2)}) async-start(bf16[4,48,64,1,128]{4,1,0,3,2:T(8,128)(2,1)} %bitcast.216), calls=%async_computation.2 | async-start | bytes 6291456 | tf_op jit(solution)/shard_map/all_to_all | solution.py:49
  141.7 71.3 %all-to-all-done.2 = bf16[4,48,64,1,128]{4,1,0,3,2:T(8,128)(2,1)} async-done(((bf16[4,48,64,1,128]{4,1,0,3,2:T(8,128)(2,1)}), bf16[4,48,64,1,128]{4,1,0,3,2:T(8,128)(2,1)}, u32[]{:S(2)}, u32[]{:S(2)}) %all-to-all-start.2) | async-done | bytes 3145760 | tf_op jit(solution)/shard_map/all_to_all | solution.py:49
  213.0 6.2 %all-to-all-start.1 = ((bf16[24,64,1,128]{3,0,2,1:T(8,128)(2,1)}), bf16[24,64,1,128]{3,0,2,1:T(8,128)(2,1)S(1)}, u32[]{:S(2)}, u32[]{:S(2)}) async-start(bf16[24,64,1,128]{3,0,2,1:T(8,128)(2,1)} %bitcast.230), calls=%async_computation.1 | async-start | bytes 786432 | tf_op jit(solution)/shard_map/all_to_all | solution.py:22
  229.4 4.2 all-to-all-done.1
  233.6 47.7 %conditional.4 = (f32[1536,1]{0,1:T(1,128)}, f32[1536,1]{0,1:T(1,128)}, f32[1536,1,128]{0,2,1:T(8,128)}) conditional(s32[]{:T(128)} %bitcast.33, () %tuple.88, (s32[3072]{0:T(1024)S(1)}, s32[]{:T(128)}, bf16[3072,1,128]{2,0,1:T(8,128)(2,1)}, bf16[1536,1,128]{2,0,1:T(8,128)(2,1)S(1)}, bf16[3072,1,128]{2,0,1:T(8,128)(2,1)}) %tuple.214), branch_computations={%region_0.0_spmd, %region_1.6_spmd} | conditional | flops 410330624 | bytes 11774295 | solution.py:99
  233.6 47.7 %while.68 = (s32[]{:T(128)}, f32[1536,1]{0,1:T(1,128)}, f32[1536,1]{0,1:T(1,128)}, f32[1536,1,128]{0,2,1:T(8,128)}, s32[3072]{0:T(1024)S(1)}, /*index=5*/s32[]{:...) while((s32[]{:T(128)}, f32[1536,1]{0,1:T(1,128)}, ...), condition=%wide.region_5.5_spmd.clone, body=%wide.region_2.4_spmd.clone.sunk | while | flops 410330624 | bytes 11774159 | solution.py:94
  245.6 2.8 fusion.136
  253.8 2.8 fusion.136
  262.1 2.8 fusion.136
  270.3 2.8 fusion.136
  278.6 2.8 fusion.136
  281.4 49.7 %conditional.5 = ((f32[1536,1]{0,1:T(1,128)}, f32[1536,1]{0,1:T(1,128)}, f32[1536,1,128]{0,2,1:T(8,128)})) conditional(s32[]{:T(128)} %bitcast.32, (f32[1536,1]{0,1:T(1,128)}, f32[1536,1]{0,1:T(1,128)}, f32[1536,1,128]{0,2,1:T(8,128)}) %conditional.4, (s32[3072]{0:T(1024)S(1)}, s32[]{:T(128)}, bf16[3072,1,128]{2,0,1:T(8,128)(2,1)}, ...), branch_computations={%region_6.7_spmd, %region_7.12_spmd} | conditional | flops 410129408 | bytes 11774291 | solution.py:99
  281.4 49.7 %while.65 = (s32[]{:T(128)}, f32[1536,1]{0,1:T(1,128)}, f32[1536,1]{0,1:T(1,128)}, f32[1536,1,128]{0,2,1:T(8,128)}, s32[3072]{0:T(1024)S(1)}, /*index=5*/s32[]{:...) while((s32[]{:T(128)}, f32[1536,1]{0,1:T(1,128)}, ...), condition=%wide.region_11.11_spmd, body=%wide.region_8.10_spmd.sunk | while | flops 410129408 | bytes 11774147 | solution.py:94
  286.8 2.8 fusion.129
  295.1 2.8 fusion.129
  303.4 2.8 fusion.129
  320.0 2.8 fusion.129
  328.3 2.8 fusion.129
  331.1 54.2 %conditional.6 = ((f32[1536,1]{0,1:T(1,128)}, f32[1536,1]{0,1:T(1,128)}, f32[1536,1,128]{0,2,1:T(8,128)})) conditional(s32[]{:T(128)} %bitcast.31, (f32[1536,1]{0,1:T(1,128)}, f32[1536,1]{0,1:T(1,128)}, f32[1536,1,128]{0,2,1:T(8,128)}) %get-tuple-element.1384, (bf16[4,64,48,1,1,128]{5,2,0,1,4,3:T(8,128)(2,1)S(1)}, ...), branch_computations={%region_12.13_spmd, %region_13.18_spmd} | conditional | flops 410129408 | bytes 27502940 | solution.py:99
  336.5 48.8 %while.66 = (s32[]{:T(128)}, f32[1536,1]{0,1:T(1,128)}, f32[1536,1]{0,1:T(1,128)}, f32[1536,1,128]{0,2,1:T(8,128)}, s32[3072]{0:T(1024)S(1)}, /*index=5*/s32[]{:...) while((s32[]{:T(128)}, f32[1536,1]{0,1:T(1,128)}, ...), condition=%wide.region_17.17_spmd, body=%wide.region_14.16_spmd.sunk | while | flops 410129408 | bytes 11774147 | solution.py:94
  341.8 2.8 fusion.123
  366.2 2.8 fusion.123
  374.4 2.8 fusion.123
  382.5 2.8 fusion.123
  385.3 55.6 %conditional.7 = (f32[1536,1]{0,1:T(1,128)}, f32[1536,1,128]{2,0,1:T(8,128)S(1)}) conditional(s32[]{:T(128)} %bitcast.30, (f32[1536,1]{0,1:T(1,128)}, f32[1536,1,128]{0,2,1:T(8,128)}) %tuple.92, (bf16[4,64,48,1,1,128]{5,2,0,1,4,3:T(8,128)(2,1)S(1)}, bf16[4,64,48,1,1,128]{5,2,0,1,4,3:T(8,128)(2,1)}, s32[4]{0:T(128)S(1)}, s32[3072]{0:T(1024)S(1)}, ...), branch_computations={%region_18.19_spmd, %region_19.24_spmd} | conditional | flops 410129408 | bytes 29075788 | solution.py:99
  390.7 48.9 %while.67 = (s32[]{:T(128)}, f32[1536,1]{0,1:T(1,128)}, f32[1536,1]{0,1:T(1,128)}, f32[1536,1,128]{0,2,1:T(8,128)}, s32[3072]{0:T(1024)S(1)}, /*index=5*/s32[]{:...) while((s32[]{:T(128)}, f32[1536,1]{0,1:T(1,128)}, ...), condition=%wide.region_23.23_spmd, body=%wide.region_20.22_spmd.sunk | while | flops 410129408 | bytes 11774147 | solution.py:94
  443.5 20.6 %all_to_all.60 = bf16[64,2,1536]{2,1,0:T(2,128)(2,1)S(1)} all-to-all(bf16[64,2,1536]{2,1,0:T(2,128)(2,1)S(1)} %reshape.274), channel_id=1, replica_groups=mesh['tm'=4,'seq'=64] {'seq'}, dimensions={0} | all-to-all | bytes 786432 | tf_op jit(solution)/shard_map/all_to_all | solution.py:103
  (200 shorter events, 188.8 us)
Async XLA Ops:
  6.5 32.7 %all-gather.5.cloned.1.call-start = ((), (), s32[]{:S(2)}) async-start(), calls=%async_computation.4 | async-start | bytes 1966080 | tf_op jit(solution)/shard_map/all_gather | solution.py:35
  44.2 85.0 %all-to-all-start = ((bf16[4,48,64,1,128]{4,1,0,3,2:T(8,128)(2,1)}), bf16[4,48,64,1,128]{4,1,0,3,2:T(8,128)(2,1)S(1)}, u32[]{:S(2)}, u32[]{:S(2)}) async-start(bf16[4,48,64,1,128]{4,1,0,3,2:T(8,128)(2,1)} %bitcast.217), calls=%async_computation | async-start | bytes 6291456 | tf_op jit(solution)/shard_map/all_to_all | solution.py:48
  55.8 30.5 %all-gather.7.cloned.1.call-start = ((), (), s32[]{:S(2)}) async-start(), calls=%async_computation.5 | async-start | bytes 1966080 | tf_op jit(solution)/shard_map/all_gather | solution.py:36
  133.2 86.1 %copy-start = (s32[4]{0:T(128)S(1)}, s32[4]{0:T(128)}, u32[]{:S(2)}) copy-start(s32[4]{0:T(128)} %param.24) | copy-start | bytes 52
  133.2 91.6 %copy-start.1 = (s32[4]{0:T(128)S(1)}, s32[4]{0:T(128)}, u32[]{:S(2)}) copy-start(s32[4]{0:T(128)} %param.25) | copy-start | bytes 52
  133.2 79.8 %all-to-all-start.2 = ((bf16[4,48,64,1,128]{4,1,0,3,2:T(8,128)(2,1)}), bf16[4,48,64,1,128]{4,1,0,3,2:T(8,128)(2,1)}, u32[]{:S(2)}, u32[]{:S(2)}) async-start(bf16[4,48,64,1,128]{4,1,0,3,2:T(8,128)(2,1)} %bitcast.216), calls=%async_computation.2 | async-start | bytes 6291456 | tf_op jit(solution)/shard_map/all_to_all | solution.py:49
  213.0 20.6 %all-to-all-start.1 = ((bf16[24,64,1,128]{3,0,2,1:T(8,128)(2,1)}), bf16[24,64,1,128]{3,0,2,1:T(8,128)(2,1)S(1)}, u32[]{:S(2)}, u32[]{:S(2)}) async-start(bf16[24,64,1,128]{3,0,2,1:T(8,128)(2,1)} %bitcast.230), calls=%async_computation.1 | async-start | bytes 786432 | tf_op jit(solution)/shard_map/all_to_all | solution.py:22
Sparse Core Ops, SparseCore 0:
  9.2 30.0 all-gather.4
  58.5 27.8 all-gather.6
where the time goes:
time: 476 us; the launch traced here: 472 us
  waiting for transfers between devices  178 us (37%)
  matrix products  103 us (22%)
  other arithmetic  79.6 us (17%)
  local copies, waits for them, and re-layouts  48.1 us (10%)
  starting transfers between devices  24.4 us (5%)
  blocking collectives  20.6 us (4%)
  between operations  18.4 us (4%)
    all_to_all x1, waiting for transfers between devices, local(): lax.all_to_all(spread_all(value_all), 'seq', split_axis=2, concat_axis=1,...  71.3 us
    dot_general x24, matrix products, advance(): jnp.einsum('qhk,khd->qhd', weights.astype(jnp.bfloat16), value_block, pre...  66.7 us
    all_to_all x1, waiting for transfers between devices, local(): lax.all_to_all(spread_all(key_all), 'seq', split_axis=2, concat_axis=1, t...  39.3 us
    dot_general x24, matrix products, advance(): jnp.einsum('qhd,khd->qhk', query_heads, key_block, preferred_element_type...  36.1 us
    all_gather x1, waiting for transfers between devices, local(): lax.all_gather(keys[None], 'tm', axis=0, tiled=True)  32 us
    add x24, other arithmetic, advance(): total = total * rescale + jnp.sum(weights, axis=2)  31.1 us
    all_gather x1, waiting for transfers between devices, local(): lax.all_gather(values[None], 'tm', axis=0, tiled=True)  29.8 us
    all_to_all x1, blocking collectives, local(): lax.all_to_all(result, 'seq', split_axis=0, concat_axis=1, tiled=True)  20.6 us
  transfers between devices with their start and end apart: 5, of which 5 were waited for; matrix products, arithmetic and copies ran while one was open for 2% of the time, Pallas kernels for 0%

commit v1 on v0

v1 whole, which is shorter than its diff:
```python
import functools

import jax
import jax.numpy as jnp
from jax import lax
from jax.experimental import pallas as pl
from jax.experimental.pallas import tpu as pltpu
from jax.sharding import PartitionSpec as P

MESH = pl.DeviceIdType.MESH
HS = 128
NX, NZ, NY = 4, 8, 4
ROWS = 48
CHUNK_DZ = ((1, 7), (2, 6), (3, 5), (0, 4))
G = len(CHUNK_DZ)
PER = 8
HALF = PER * ROWS
KEYS = 2 * HALF
NQ = 8 * ROWS
SCALE = HS ** (-0.5) * 1.4426950408889634
TK = 256
FLAG_COMPUTE = True
FLAG_Y = True
FLAG_D2D = True
FLAG_Q = True
FLAG_O = True
Q_AT = 1
ORDER_DX = (0, 1, 2, 3)


def lanesum(p):
    total = p[:, :HS]
    for at in range(HS, p.shape[1], HS):
        total = total + p[:, at : at + HS]
    return total


def kernel(rank_ref, count_ref, q_ref, k_ref, v_ref, out_ref, kv0, kv1, kv2, kv3, qb, qs, ob, os, m_s, l_s, a_s,
           a2a_sem, lr_sem, far_sem, d2d_sem, q_sem, o_sem, kv_send, q_send, o_send, y_send, f_send, d_send):
    kvb = (kv0, kv1, kv2, kv3)
    y = lax.axis_index("tm")
    s = lax.axis_index("seq")
    h = s // 2
    c = s % 2
    x = h // NZ
    z = h % NZ

    def at(dx, dy, dz):
        hd = ((x + dx) % NX) * NZ + (z + dz) % NZ
        return (y + dy) % NY, hd

    def send_kv(g):
        for i, dz in enumerate(CHUNK_DZ[g]):
            for n, dx in enumerate(ORDER_DX):
                slot = i * NX + n
                _, hd = at(dx, 0, dz)
                cols = pl.ds(pl.multiple_of(hd * HS, HS), HS)
                for j, ref in enumerate((k_ref, v_ref)):
                    src = ref.at[:, cols]
                    dst = kvb[g].at[0, j, pl.ds(slot * ROWS, ROWS), :]
                    if dx == 0 and dz == 0:
                        pltpu.make_async_copy(src, dst, a2a_sem.at[g]).start()
                    else:
                        pltpu.make_async_remote_copy(
                            src, dst, kv_send, a2a_sem.at[g], device_id=(y, 2 * hd + c), device_id_type=MESH
                        ).start()

    def send_q():
        for dz in range(NZ):
            for dx in range(NX):
                dy = dz % NY
                yd, hd = at(dx, dy, dz)
                src = q_ref.at[:, pl.ds(pl.multiple_of(hd * HS, HS), HS)]
                dst = qb.at[dy, pl.ds(((dz // NY) * NX + dx) * ROWS, ROWS), :]
                if dx == 0 and dz == 0:
                    pltpu.make_async_copy(src, dst, q_sem).start()
                else:
                    pltpu.make_async_remote_copy(
                        src, dst, q_send, q_sem, device_id=(yd, 2 * hd + c), device_id_type=MESH
                    ).start()

    def send_o(dy):
        cols = pl.ds(pl.multiple_of(h * HS, HS), HS)
        for dz in (dy, dy + NY):
            for dx in range(NX):
                yd, hd = at(-dx, -dy, -dz)
                src = ob.at[dy, pl.ds(((dz // NY) * NX + dx) * ROWS, ROWS), :]
                dst = out_ref.at[:, cols]
                if dx == 0 and dz == 0:
                    pltpu.make_async_copy(src, dst, o_sem).start()
                else:
                    pltpu.make_async_remote_copy(
                        src, dst, o_send, o_sem, device_id=(yd, 2 * hd + c), device_id_type=MESH
                    ).start()

    def wait(ref, sem):
        pltpu.make_async_copy(ref, ref, sem).wait()

    def half(g, d, j=None):
        if j is None:
            return kvb[g].at[d, :, pl.ds(0, HALF), :]
        return kvb[g].at[d, j, pl.ds(0, HALF), :]

    def other(g, d):
        return kvb[g].at[d, :, pl.ds(HALF, HALF), :]

    def y_copy(g, to_right):
        step, d = (1, 3) if to_right else (-1, 1)
        return pltpu.make_async_remote_copy(
            half(g, 0), half(g, d), y_send.at[g, int(to_right)], lr_sem.at[g, int(to_right)],
            device_id=((y + step) % NY, s), device_id_type=MESH)

    def far_copy(g, to_right):
        step, d, j = (1, 3, 0) if to_right else (-1, 1, 1)
        return pltpu.make_async_remote_copy(
            half(g, d, j), half(g, 2, j), f_send.at[g, int(to_right)], far_sem.at[g, int(to_right)],
            device_id=((y + step) % NY, s), device_id_type=MESH)

    def d2d_copy(g, d):
        return pltpu.make_async_remote_copy(
            half(g, d), other(g, d), d_send.at[g, d], d2d_sem.at[g, d],
            device_id=(y, s + 1 - 2 * c), device_id_type=MESH)

    def stage_a(g):
        wait(half(g, 0), a2a_sem.at[g])
        if FLAG_Y:
            y_copy(g, True).start()
            y_copy(g, False).start()
        if FLAG_D2D:
            d2d_copy(g, 0).start()

    def stage_b(g):
        for right in (True, False):
            if FLAG_Y:
                y_copy(g, right).wait_recv()
                far_copy(g, right).start()
            if FLAG_D2D:
                d2d_copy(g, 3 if right else 1).start()

    def stage_c(g):
        if FLAG_Y:
            far_copy(g, True).wait_recv()
            far_copy(g, False).wait_recv()
        if FLAG_D2D:
            d2d_copy(g, 2).start()

    def stage_d(g):
        if FLAG_D2D:
            for d in range(4):
                d2d_copy(g, d).wait_recv()

    ranks = [rank_ref[t] for t in range(4)]

    def order(r):
        return lax.rem(sum(jnp.where(ranks[t] == r, t, 0) for t in range(1, 4)), 4)

    def positions(g):
        col = lax.broadcasted_iota(jnp.int32, (8, KEYS), 1)
        pos = col
        for m in range(2):
            core = c if m == 0 else 1 - c
            for i, dz in enumerate(CHUNK_DZ[g]):
                for n, dx in enumerate(ORDER_DX):
                    first = m * HALF + (i * NX + n) * ROWS
                    _, hd = at(-dx, 0, -dz)
                    base = (2 * hd + core) * ROWS - first
                    pos = jnp.where((col >= first) & (col < first + ROWS), col + base, pos)
        return pos[:1]

    def compute(g):
        pos = positions(g)
        for j in range(4):
            t = order(j)
            d = lax.rem(t - y + 4, 4)
            limit = count_ref[t]
            rows = pl.ds(j * NQ, (4 - j) * NQ)
            for at_key in range(0, KEYS, TK):
                k = kvb[g][d, 0, at_key : at_key + TK, :]
                v = kvb[g][d, 1, at_key : at_key + TK, :]
                live = pos[:, at_key : at_key + TK] < limit
                scores = lax.dot_general(qs[rows, :], k, (((1,), (1,)), ((), ())), preferred_element_type=jnp.float32)
                scores = jnp.where(live, scores, -1e30)
                before = m_s[rows, :]
                upper = jnp.maximum(before, jnp.max(scores, axis=1, keepdims=True) * SCALE)
                rescale = jnp.exp2(before - upper)
                weights = jnp.exp2(scores * SCALE - jnp.concatenate([upper] * (TK // HS), axis=1))
                l_s[rows, :] = l_s[rows, :] * rescale + lanesum(weights)
                a_s[rows, :] = a_s[rows, :] * rescale + jnp.dot(
                    weights.astype(jnp.bfloat16), v, preferred_element_type=jnp.float32)
                m_s[rows, :] = upper

    for g in range(G):
        if g == Q_AT and FLAG_Q:
            send_q()
        send_kv(g)
    if Q_AT >= G and FLAG_Q:
        send_q()
    if FLAG_COMPUTE:
        m_s[...] = jnp.full(m_s.shape, -1e30, jnp.float32)
        l_s[...] = jnp.zeros(l_s.shape, jnp.float32)
        a_s[...] = jnp.zeros(a_s.shape, jnp.float32)
    for step in range(G + 3):
        if step < G:
            stage_a(step)
        if 0 <= step - 1 < G:
            stage_b(step - 1)
        if 0 <= step - 2 < G:
            stage_c(step - 2)
        if 0 <= step - 3 < G:
            if step == 3 and FLAG_Q:
                wait(qb, q_sem)
                if FLAG_COMPUTE:
                    for r in range(4):
                        qs[pl.ds(r * NQ, NQ), :] = qb[lax.rem(y - order(r) + 4, 4)]
            stage_d(step - 3)
            if FLAG_COMPUTE:
                compute(step - 3)
    if FLAG_COMPUTE:
        for r in range(4):
            rows = pl.ds(r * NQ, NQ)
            os[r] = (a_s[rows, :] / jnp.sum(l_s[rows, :], axis=1, keepdims=True)).astype(jnp.bfloat16)
        for dy in range(4):
            t = lax.rem(y - dy + 4, 4)
            ob[dy] = os[rank_ref[t]]
    if FLAG_O:
        for dy in range(4):
            send_o(dy)
        wait(out_ref, o_sem)
    else:
        out_ref[...] = q_ref[...]
    sent = k_ref.at[:, pl.ds(0, 31 * HS)]
    wait(sent, kv_send)
    wait(sent, kv_send)
    if FLAG_Q:
        wait(sent, q_send)
    if FLAG_O:
        wait(sent, o_send)
    for g in range(G):
        for right in (True, False):
            if FLAG_Y:
                y_copy(g, right).wait_send()
                far_copy(g, right).wait_send()
        if FLAG_D2D:
            for d in range(4):
                d2d_copy(g, d).wait_send()


def local(queries, keys, values, span_rank, token_counts):
    vmem = pl.BlockSpec(memory_space=pltpu.VMEM)
    smem = pl.BlockSpec(memory_space=pltpu.SMEM)
    dma = pltpu.SemaphoreType.DMA
    return pl.pallas_call(
        kernel,
        out_shape=jax.ShapeDtypeStruct(queries.shape, jnp.bfloat16),
        in_specs=[smem, smem, vmem, vmem, vmem],
        out_specs=vmem,
        scratch_shapes=[
            *[pltpu.VMEM((4, 2, KEYS, HS), jnp.bfloat16)] * G,
            pltpu.VMEM((4, NQ, HS), jnp.bfloat16),
            pltpu.VMEM((4 * NQ, HS), jnp.bfloat16),
            pltpu.VMEM((4, NQ, HS), jnp.bfloat16),
            pltpu.VMEM((4, NQ, HS), jnp.bfloat16),
            pltpu.VMEM((4 * NQ, HS), jnp.float32),
            pltpu.VMEM((4 * NQ, HS), jnp.float32),
            pltpu.VMEM((4 * NQ, HS), jnp.float32),
            dma((G,)), dma((G, 2)), dma((G, 2)), dma((G, 4)), dma, dma, dma, dma, dma, dma((G, 2)), dma((G, 2)), dma((G, 4)),
        ],
        compiler_params=pltpu.CompilerParams(has_side_effects=True, vmem_limit_bytes=48 * 2**20),
    )(span_rank, token_counts, queries, keys, values)


def solution(mesh):
    spec = P(("tm", "seq"), None)
    return jax.shard_map(
        local, mesh=mesh, in_specs=(spec, spec, spec, P(), P()), out_specs=spec, check_vma=False
    )
```

time: 476 us -> 92.2 us (0.19)
  the two profiles are of different devices: /device:TPU:23 before, /device:TPU:32 now
where the time goes in v1:
time: 92.2 us; the launch traced here: 92 us
  Pallas kernels  87 us (94%)
  local copies, waits for them, and re-layouts  5.04 us (5%)
    pallas_call x1, Pallas kernels, local(): pl.pallas_call(kernel, out_shape=jax.ShapeDtypeStruct(queries.shape, jnp....  87 us
    unnamed x11, local copies, waits for them, and re-layouts  5.04 us

profile of v1, /device:TPU:32, one launch (start us, length us, event | category | flops | bytes accessed | tf_op | source)
XLA Modules:
  0.0 92.0 jit_solution(3102338353567894111)
XLA Ops:
  0.0 0.0 copy-start
  0.0 1.0 %copy-done = bf16[48,4096]{1,0:T(8,128)(2,1)S(1)} copy-done((bf16[48,4096]{1,0:T(8,128)(2,1)S(1)}, bf16[48,4096]{1,0:T(8,128)(2,1)}, u32[]{:S(2)}) %copy-start) | copy-done | bytes 393240
  1.0 0.0 copy-start.1
  1.0 1.0 %copy-done.1 = bf16[48,4096]{1,0:T(8,128)(2,1)S(1)} copy-done((bf16[48,4096]{1,0:T(8,128)(2,1)S(1)}, bf16[48,4096]{1,0:T(8,128)(2,1)}, u32[]{:S(2)}) %copy-start.1) | copy-done | bytes 393240
  2.0 0.0 copy-start.2
  2.0 1.0 %copy-done.2 = bf16[48,4096]{1,0:T(8,128)(2,1)S(1)} copy-done((bf16[48,4096]{1,0:T(8,128)(2,1)S(1)}, bf16[48,4096]{1,0:T(8,128)(2,1)}, u32[]{:S(2)}) %copy-start.2) | copy-done | bytes 393240
  3.0 0.0 copy-start.3
  3.0 0.7 copy-done.3
  3.6 0.0 copy-start.4
  3.6 0.7 copy-done.4
  4.3 87.0 %shard_map.55 = bf16[48,4096]{1,0:T(8,128)(2,1)S(1)} custom-call(s32[4]{0:T(128)S(1)} %copy-done.3, s32[4]{0:T(128)S(1)} %copy-done.4, bf16[48,4096]{1,0:T(8,128)(2,1)S(1)} %copy-done, bf16[48,4096]{1,0:T(8,128)(2,1)S(1)} %copy-done.1, bf16[48,4096]{1,0:T(8,128)(2,1)S(1)} %copy-done.2), custom_call_target="tpu_custom_call" | custom-call | tf_op jit(solution)/shard_map/pallas_call | solution.py:252
  91.3 0.7 copy.7
Async XLA Ops:
  0.0 1.0 %copy-start = (bf16[48,4096]{1,0:T(8,128)(2,1)S(1)}, bf16[48,4096]{1,0:T(8,128)(2,1)}, u32[]{:S(2)}) copy-start(bf16[48,4096]{1,0:T(8,128)(2,1)} %q_ref.1) | copy-start | bytes 1179652
  1.0 1.0 %copy-start.1 = (bf16[48,4096]{1,0:T(8,128)(2,1)S(1)}, bf16[48,4096]{1,0:T(8,128)(2,1)}, u32[]{:S(2)}) copy-start(bf16[48,4096]{1,0:T(8,128)(2,1)} %k_ref.1) | copy-start | bytes 1179652
  2.0 1.0 %copy-start.2 = (bf16[48,4096]{1,0:T(8,128)(2,1)S(1)}, bf16[48,4096]{1,0:T(8,128)(2,1)}, u32[]{:S(2)}) copy-start(bf16[48,4096]{1,0:T(8,128)(2,1)} %v_ref.1) | copy-start | bytes 1179652
  3.0 0.7 copy-start.3
  3.6 0.7 copy-start.4

commit v2 on v0

v2 whole, which is shorter than its diff:
```python
import functools

import jax
import jax.numpy as jnp
from jax import lax
from jax.experimental import pallas as pl
from jax.experimental.pallas import tpu as pltpu
from jax.sharding import PartitionSpec as P

MESH = pl.DeviceIdType.MESH
HS = 128
NX, NZ, NY = 4, 8, 4
ROWS = 48
UNIT = NX * ROWS
HALF = 2 * UNIT
KEYS = 2 * HALF
NQ = 4 * ROWS
SCALE = HS ** (-0.5) * 1.4426950408889634
TK = 256
UNITS = (0, 1, 7, 2, 6, 4, 3, 5)
HALVES = {"n": (0, 1, 6, 7), "f": (4, 5, 2, 3)}
SENDS = (0, 1, 7, 2, 6, "n", "f", 4, 3, 5)
STEPS = (
    "a0", "a1", "a7", "a2", "a6", "b0", "b1", "b7", "b2", "b6", "f0", "f1",
    "qn", "qf", "c0b", "a4", "f7", "f2", "a3", "a5", "b4", "c1b", "b3", "b5",
    "f6", "f4", "c2b", "f3", "f5", "c3b", "of", "on",
)
PEERS = sorted(
    {(dx, dy, 0) for dx in range(NX) for dy in range(NY)}
    | {(dx, 0, dz) for dx in range(NX) for dz in range(NZ)}
    | {(dx, dz % NY, dz) for dx in range(NX) for dz in range(NZ)}
)


def far(offset):
    return sum(min(d, n - d) for d, n in zip(offset, (NX, NY, NZ)))


def lanesum(p):
    total = p[:, :HS]
    for at in range(HS, p.shape[1], HS):
        total = total + p[:, at : at + HS]
    return total


def kernel(rank_hbm, count_hbm, q_hbm, k_hbm, v_hbm, out_ref, kv0, kv1, kv2, kv3, q_ref, k_ref, v_ref,
           rank_ref, count_ref, qbn, qbf, qs, obn, obf, osn, osf, m_s, l_s, a_s,
           in_sem, a_sem, b_sem, f_sem, d_sem, q_sem, o_sem, kv_send, q_send, o_send, y_send, f_send, d_send):
    kvb = (kv0, kv1, kv2, kv3)
    qbs, obs, oss = {"n": qbn, "f": qbf}, {"n": obn, "f": obf}, {"n": osn, "f": osf}
    number = {"n": 0, "f": 1}
    y = lax.axis_index("tm")
    s = lax.axis_index("seq")
    h = s // 2
    c = s % 2
    x = h // NZ
    z = h % NZ

    def at(dx, dy, dz):
        hd = ((x + dx) % NX) * NZ + (z + dz) % NZ
        return (y + dy) % NY, hd

    def remote(src, dst, send, recv, where):
        return pltpu.make_async_remote_copy(src, dst, send, recv, device_id=where, device_id_type=MESH)

    def wait(ref, sem):
        pltpu.make_async_copy(ref, ref, sem).wait()

    def place(dz):
        n = UNITS.index(dz)
        return n // 2, (n % 2) * UNIT

    def mine(dz, spans):
        n, row = place(dz)
        return kvb[n].at[spans, :, pl.ds(row, UNIT), :]

    def theirs(dz, spans):
        n, row = place(dz)
        return kvb[n].at[spans, :, pl.ds(HALF + row, UNIT), :]

    ALL, OWN = pl.ds(0, 4), pl.ds(0, 1)

    def send_kv(dz):
        n, row = place(dz)
        for dy in (1, 3, 0) if dz == 0 else (0,):
            for dx in range(NX):
                yd, hd = at(dx, dy, dz)
                cols = pl.ds(pl.multiple_of(hd * HS, HS), HS)
                for j, ref in enumerate((k_ref, v_ref)):
                    src = ref.at[:, cols]
                    dst = kvb[n].at[(NY - dy) % NY, j, pl.ds(row + dx * ROWS, ROWS), :]
                    if (dx, dy, dz) == (0, 0, 0):
                        pltpu.make_async_copy(src, dst, a_sem.at[0]).start()
                    else:
                        recv = b_sem.at[0, dy] if dy else a_sem.at[dz]
                        remote(src, dst, kv_send, recv, (yd, 2 * hd + c)).start()

    def send_q(half):
        for dz in HALVES[half]:
            for dx in range(NX):
                dy = dz % NY
                yd, hd = at(dx, dy, dz)
                src = q_ref.at[:, pl.ds(pl.multiple_of(hd * HS, HS), HS)]
                dst = qbs[half].at[dy, pl.ds(dx * ROWS, ROWS), :]
                if (dx, dz) == (0, 0):
                    pltpu.make_async_copy(src, dst, q_sem.at[0]).start()
                else:
                    remote(src, dst, q_send, q_sem.at[number[half]], (yd, 2 * hd + c)).start()

    def sort_q(half):
        wait(qbs[half], q_sem.at[number[half]])
        for r in range(4):
            qs[pl.ds((2 * r + number[half]) * NQ, NQ), :] = qbs[half][lax.rem(y - order(r) + 4, 4)]

    def send_o(half):
        cols = pl.ds(pl.multiple_of(h * HS, HS), HS)
        for dz in HALVES[half]:
            for dx in range(NX):
                dy = dz % NY
                yd, hd = at(-dx, -dy, -dz)
                src = obs[half].at[dy, pl.ds(dx * ROWS, ROWS), :]
                dst = out_ref.at[:, cols]
                if (dx, dz) == (0, 0):
                    pltpu.make_async_copy(src, dst, o_sem).start()
                else:
                    remote(src, dst, o_send, o_sem, (yd, 2 * hd + c)).start()

    def finish(half):
        for r in range(4):
            rows = pl.ds((2 * r + number[half]) * NQ, NQ)
            total = jnp.sum(l_s[rows, :], axis=1, keepdims=True)
            oss[half][r] = (a_s[rows, :] / total).astype(jnp.bfloat16)
        for dy in range(NY):
            obs[half][dy] = oss[half][lax.rem(rank_ref[lax.rem(y - dy + 4, 4)], 4)]

    def y_copy(dz, dy):
        return remote(mine(dz, OWN), mine(dz, pl.ds(NY - dy, 1)), y_send.at[dz, dy], b_sem.at[dz, dy], ((y + dy) % NY, s))

    def f_copy(dz, dy):
        n, row = place(dz)
        j = 0 if dy == 1 else 1
        src = kvb[n].at[NY - dy, j, pl.ds(row, UNIT), :]
        dst = kvb[n].at[2, j, pl.ds(row, UNIT), :]
        return remote(src, dst, f_send.at[dz, dy], f_sem.at[dz], ((y + dy) % NY, s))

    def d_copy(dz, d):
        return remote(mine(dz, pl.ds(d, 1)), theirs(dz, pl.ds(d, 1)), d_send.at[dz, d], d_sem.at[dz], (y, s + 1 - 2 * c))

    def stage_a(dz):
        wait(mine(dz, OWN), a_sem.at[dz])
        if dz:
            for dy in (1, 3):
                y_copy(dz, dy).start()
        d_copy(dz, 0).start()

    def stage_b(dz):
        for dy in (1, 3):
            wait(mine(dz, pl.ds(NY - dy, 1)), b_sem.at[dz, dy])
            f_copy(dz, dy).start()
            d_copy(dz, NY - dy).start()

    def stage_f(dz):
        wait(mine(dz, pl.ds(2, 1)), f_sem.at[dz])
        d_copy(dz, 2).start()

    def order(r):
        return lax.rem(sum(jnp.where(rank_ref[t] == r, t, 0) for t in range(1, 4)), 4)

    def positions(n):
        col = lax.broadcasted_iota(jnp.int32, (8, KEYS), 1)
        pos = col
        for m in range(2):
            core = c if m == 0 else 1 - c
            for i, dz in enumerate(UNITS[2 * n : 2 * n + 2]):
                for dx in range(NX):
                    first = m * HALF + i * UNIT + dx * ROWS
                    _, hd = at(-dx, 0, -dz)
                    base = (2 * hd + core) * ROWS - first
                    pos = jnp.where((col >= first) & (col < first + ROWS), col + base, pos)
        return pos[:1]

    def compute(n, half):
        pos = positions(n)
        for j in range(4):
            t = order(j)
            d = lax.rem(t - y + 4, 4)
            limit = count_ref[t]
            if half == "b":
                pieces = [pl.ds(2 * j * NQ, (4 - j) * 2 * NQ)]
            else:
                pieces = [pl.ds((2 * r + number[half]) * NQ, NQ) for r in range(j, 4)]

            def get(ref):
                return jnp.concatenate([ref[rows, :] for rows in pieces], axis=0)

            def put(ref, new):
                first = 0
                for rows in pieces:
                    ref[rows, :] = new[first : first + rows.size]
                    first += rows.size

            queries = get(qs)
            for at_key in range(0, KEYS, TK):
                k = kvb[n][d, 0, at_key : at_key + TK, :]
                v = kvb[n][d, 1, at_key : at_key + TK, :]
                live = pos[:, at_key : at_key + TK] < limit
                scores = lax.dot_general(queries, k, (((1,), (1,)), ((), ())), preferred_element_type=jnp.float32)
                scores = jnp.where(live, scores, -1e30)
                before = get(m_s)
                upper = jnp.maximum(before, jnp.max(scores, axis=1, keepdims=True) * SCALE)
                rescale = jnp.exp2(before - upper)
                weights = jnp.exp2(scores * SCALE - jnp.concatenate([upper] * (TK // HS), axis=1))
                put(l_s, get(l_s) * rescale + lanesum(weights))
                put(a_s, get(a_s) * rescale + jnp.dot(
                    weights.astype(jnp.bfloat16), v, preferred_element_type=jnp.float32))
                put(m_s, upper)

    ready = set()

    def run_step(step):
        kind, what = step[0], step[1:]
        if kind == "a":
            stage_a(int(what))
        elif kind == "b":
            stage_b(int(what))
        elif kind == "f":
            stage_f(int(what))
        elif kind == "q":
            sort_q(what)
        elif kind == "c":
            n = int(what[0])
            if n not in ready:
                for dz in UNITS[2 * n : 2 * n + 2]:
                    wait(theirs(dz, ALL), d_sem.at[dz])
            ready.add(n)
            compute(n, what[1])
        elif kind == "o":
            finish(what)
            send_o(what)

    barrier = pltpu.get_barrier_semaphore()
    for dx, dy, dz in sorted(PEERS, key=far, reverse=True):
        if (dx, dy, dz) != (0, 0, 0):
            yd, hd = at(dx, dy, dz)
            pl.semaphore_signal(barrier, inc=1, device_id=(yd, 2 * hd + c), device_id_type=MESH)
    pl.semaphore_signal(barrier, inc=1, device_id=(y, s + 1 - 2 * c), device_id_type=MESH)
    loads = [
        pltpu.make_async_copy(src, dst, in_sem.at[i])
        for i, (src, dst) in enumerate(
            ((k_hbm, k_ref), (v_hbm, v_ref), (q_hbm, q_ref), (rank_hbm, rank_ref), (count_hbm, count_ref))
        )
    ]
    for load in loads:
        load.start()
    for load in loads:
        load.wait()
    pl.semaphore_wait(barrier, len(PEERS))

    for what in SENDS:
        if what in HALVES:
            send_q(what)
        else:
            send_kv(what)
    m_s[...] = jnp.full(m_s.shape, -1e30, jnp.float32)
    l_s[...] = jnp.zeros(l_s.shape, jnp.float32)
    a_s[...] = jnp.zeros(a_s.shape, jnp.float32)
    for step in STEPS:
        run_step(step)
    wait(out_ref, o_sem)
    sent = k_ref.at[:, pl.ds(0, 31 * HS)]
    for _ in range(2):
        wait(sent, kv_send)
        wait(k_ref.at[:, pl.ds(0, 8 * HS)], kv_send)
    wait(sent, q_send)
    wait(sent, o_send)
    for dz in UNITS:
        for dy in (1, 3):
            if dz:
                y_copy(dz, dy).wait_send()
            f_copy(dz, dy).wait_send()
        for d in range(NY):
            d_copy(dz, d).wait_send()


def local(queries, keys, values, span_rank, token_counts):
    vmem = pl.BlockSpec(memory_space=pltpu.VMEM)
    hbm = pl.BlockSpec(memory_space=pltpu.HBM)
    dma = pltpu.SemaphoreType.DMA
    shape = queries.shape
    return pl.pallas_call(
        kernel,
        out_shape=jax.ShapeDtypeStruct(shape, jnp.bfloat16),
        in_specs=[hbm] * 5,
        out_specs=vmem,
        scratch_shapes=[
            *[pltpu.VMEM((4, 2, KEYS, HS), jnp.bfloat16)] * 4,
            *[pltpu.VMEM(shape, jnp.bfloat16)] * 3,
            pltpu.SMEM((4,), jnp.int32),
            pltpu.SMEM((4,), jnp.int32),
            *[pltpu.VMEM((4, NQ, HS), jnp.bfloat16)] * 2,
            pltpu.VMEM((8 * NQ, HS), jnp.bfloat16),
            *[pltpu.VMEM((4, NQ, HS), jnp.bfloat16)] * 4,
            *[pltpu.VMEM((8 * NQ, HS), jnp.float32)] * 3,
            dma((5,)), dma((8,)), dma((8, 4)), dma((8,)), dma((8,)), dma((2,)), dma, dma, dma, dma, dma((8, 4)), dma((8, 4)), dma((8, 4)),
        ],
        compiler_params=pltpu.CompilerParams(
            has_side_effects=True, collective_id=0, vmem_limit_bytes=48 * 2**20
        ),
    )(span_rank, token_counts, queries, keys, values)


def solution(mesh):
    spec = P(("tm", "seq"), None)
    return jax.shard_map(
        local, mesh=mesh, in_specs=(spec, spec, spec, P(), P()), out_specs=spec, check_vma=False
    )
```

time: 476 us -> 84.7 us (0.18)
  the two profiles are of different devices: /device:TPU:23 before, /device:TPU:32 now
where the time goes in v2:
time: 84.7 us; the launch traced here: 83.9 us
  Pallas kernels  78.8 us (93%)
  local copies, waits for them, and re-layouts  5.04 us (6%)
    pallas_call x1, Pallas kernels, local(): pl.pallas_call(kernel, out_shape=jax.ShapeDtypeStruct(shape, jnp.bfloat16...  78.8 us
    unnamed x11, local copies, waits for them, and re-layouts  5.04 us

profile of v2, /device:TPU:32, one launch (start us, length us, event | category | flops | bytes accessed | tf_op | source)
XLA Modules:
  0.0 83.9 jit_solution(5062714535907668937)
XLA Ops:
  0.0 0.0 copy-start
  0.0 1.0 %copy-done = bf16[48,4096]{1,0:T(8,128)(2,1)S(1)} copy-done((bf16[48,4096]{1,0:T(8,128)(2,1)S(1)}, bf16[48,4096]{1,0:T(8,128)(2,1)}, u32[]{:S(2)}) %copy-start) | copy-done | bytes 393240
  1.0 0.0 copy-start.1
  1.0 1.0 %copy-done.1 = bf16[48,4096]{1,0:T(8,128)(2,1)S(1)} copy-done((bf16[48,4096]{1,0:T(8,128)(2,1)S(1)}, bf16[48,4096]{1,0:T(8,128)(2,1)}, u32[]{:S(2)}) %copy-start.1) | copy-done | bytes 393240
  2.0 0.0 copy-start.2
  2.0 1.0 %copy-done.2 = bf16[48,4096]{1,0:T(8,128)(2,1)S(1)} copy-done((bf16[48,4096]{1,0:T(8,128)(2,1)S(1)}, bf16[48,4096]{1,0:T(8,128)(2,1)}, u32[]{:S(2)}) %copy-start.2) | copy-done | bytes 393240
  3.0 0.0 copy-start.3
  3.0 0.7 copy-done.3
  3.6 0.0 copy-start.4
  3.6 0.7 copy-done.4
  4.3 78.8 %shard_map.55 = bf16[48,4096]{1,0:T(8,128)(2,1)S(1)} custom-call(s32[4]{0:T(128)S(1)} %copy-done.3, s32[4]{0:T(128)S(1)} %copy-done.4, bf16[48,4096]{1,0:T(8,128)(2,1)S(1)} %copy-done, bf16[48,4096]{1,0:T(8,128)(2,1)S(1)} %copy-done.1, bf16[48,4096]{1,0:T(8,128)(2,1)S(1)} %copy-done.2), custom_call_target="tpu_custom_call" | custom-call | tf_op jit(solution)/shard_map/pallas_call | solution.py:290
  83.1 0.7 copy.7
Async XLA Ops:
  0.0 1.0 %copy-start = (bf16[48,4096]{1,0:T(8,128)(2,1)S(1)}, bf16[48,4096]{1,0:T(8,128)(2,1)}, u32[]{:S(2)}) copy-start(bf16[48,4096]{1,0:T(8,128)(2,1)} %q_hbm.1) | copy-start | bytes 1179652
  1.0 1.0 %copy-start.1 = (bf16[48,4096]{1,0:T(8,128)(2,1)S(1)}, bf16[48,4096]{1,0:T(8,128)(2,1)}, u32[]{:S(2)}) copy-start(bf16[48,4096]{1,0:T(8,128)(2,1)} %k_hbm.1) | copy-start | bytes 1179652
  2.0 1.0 %copy-start.2 = (bf16[48,4096]{1,0:T(8,128)(2,1)S(1)}, bf16[48,4096]{1,0:T(8,128)(2,1)}, u32[]{:S(2)}) copy-start(bf16[48,4096]{1,0:T(8,128)(2,1)} %v_hbm.1) | copy-start | bytes 1179652
  3.0 0.7 copy-start.3
  3.6 0.7 copy-start.4
